TPU v7x, 256 devices: a whole 4x4x8 slice. The times are simulated.
256 devices in a mesh: dp: 8 (over x, core), seq: 32 (over z, y).
Axes of the slice: x: 4, y: 4, z: 8, core: 2. Of those that a mesh axis runs over, the one named last changes fastest.
Arguments:
- queries: bfloat16 [8, 32, 256, 1536], P('dp', 'seq'), may hold values from -6 to 6
- keys_spatial: bfloat16 [8, 32, 256, 1536], P('dp', 'seq'), may hold values from -6 to 6
- values_spatial: bfloat16 [8, 32, 256, 1536], P('dp', 'seq'), may hold values from -6 to 6
- temporal_keys: bfloat16 [8, 32, 256, 1536], P('dp', 'seq'), may hold values from -6 to 6
- temporal_values: bfloat16 [8, 32, 256, 1536], P('dp', 'seq'), may hold values from -6 to 6
- tile_mask: int32 [8, 32, 2, 2], P('dp', 'seq'), may hold values 0 or 1
- query_weight: bfloat16 [1536, 1536], P('seq'), may hold values from -0.15625 to 0.15625
- out_grad: bfloat16 [8, 32, 256, 1536], P('dp', None, 'seq'), may hold values from -6 to 6
Outputs:
- d_queries: bfloat16 [8, 32, 256, 1536], P('dp', 'seq')
- d_keys_spatial: bfloat16 [8, 32, 256, 1536], P('dp', 'seq')
- d_values_spatial: bfloat16 [8, 32, 256, 1536], P('dp', 'seq')
- d_temporal_keys: bfloat16 [8, 32, 256, 1536], P('dp', 'seq')
- d_temporal_values: bfloat16 [8, 32, 256, 1536], P('dp', 'seq')
- d_weight: bfloat16 [1536, 1536], P('seq')
All inputs are finite; a program needn't handle non-finite values. No bound on the sum of `tile_mask` on one device may be relied on, other than what follows from the above.
Results may differ from a plain program's by a relative error of at most 0.03.
Values may be sent and summed in bfloat16 or wider, within the bound.
A program may use at most 192 MiB of HBM per device.

v0:
```python
import math

import jax
import jax.numpy as jnp
from jax import lax
from jax.sharding import PartitionSpec as P

HEADS = 12
HEAD_DIM = 128
TILE = 128


def head_rmsnorm(values_in):
    floats = values_in.astype(jnp.float32)
    floats = floats.reshape(floats.shape[:-1] + (HEADS, HEAD_DIM))
    scaled = floats * lax.rsqrt(jnp.mean(floats * floats, axis=-1, keepdims=True) + 1e-06)
    return scaled.astype(jnp.bfloat16)


def dense_frame(queries, keys_in, values_in, allowed):
    patches = queries.shape[0]
    query_norm = head_rmsnorm(queries)
    key_norm = head_rmsnorm(keys_in)
    value_heads = values_in.reshape(patches, HEADS, HEAD_DIM)
    scores = jnp.einsum(
        "phd,khd->hpk", query_norm, key_norm, preferred_element_type=jnp.float32
    ) / math.sqrt(HEAD_DIM)
    full_mask = jnp.repeat(jnp.repeat(allowed, TILE, axis=0), TILE, axis=1)
    exps = jnp.exp(scores) * full_mask[None]
    weights = (exps / jnp.sum(exps, axis=-1, keepdims=True)).astype(jnp.bfloat16)
    result = jnp.einsum("hpk,khd->phd", weights, value_heads, preferred_element_type=jnp.float32)
    return result.astype(jnp.bfloat16).reshape(patches, HEADS * HEAD_DIM)


def temporal_block(projected, keys_in, values_in):
    dims_in = projected.shape
    query_norm = head_rmsnorm(projected)
    key_norm = head_rmsnorm(keys_in)
    value_heads = values_in.reshape(dims_in[:-1] + (HEADS, HEAD_DIM))
    scores = jnp.einsum(
        "cfphd,cgphd->cphfg", query_norm, key_norm, preferred_element_type=jnp.float32
    ) / math.sqrt(HEAD_DIM)
    exps = jnp.exp(scores)
    weights = (exps / jnp.sum(exps, axis=-1, keepdims=True)).astype(jnp.bfloat16)
    result = jnp.einsum(
        "cphfg,cgphd->cfphd", weights, value_heads, preferred_element_type=jnp.float32
    )
    return result.astype(jnp.bfloat16).reshape(dims_in)


def per_device(
    queries,
    keys_spatial,
    values_spatial,
    temporal_keys,
    temporal_values,
    tile_mask,
    query_weight,
    out_grad,
):
    clip_count, frame_count, patches, width = queries.shape
    tile_count = patches // TILE
    diagonal = jnp.eye(tile_count, dtype=bool)
    allowed = jnp.logical_or(tile_mask == 1, diagonal).astype(jnp.float32)
    allowed = allowed.reshape(clip_count * frame_count, tile_count, tile_count)

    def spatial_all(first_in, second_in, third_in):

        def per_frame(inputs):
            return dense_frame(inputs[0], inputs[1], inputs[2], inputs[3])

        framed = lax.map(
            per_frame,
            (
                first_in.reshape(-1, patches, width),
                second_in.reshape(-1, patches, width),
                third_in.reshape(-1, patches, width),
                allowed,
            ),
        )
        return framed.reshape(clip_count, frame_count, patches, width)

    spatial_out, spatial_back = jax.vjp(spatial_all, queries, keys_spatial, values_spatial)
    full_weight = lax.all_gather(query_weight, "seq", axis=0, tiled=True)
    spatial_patch, keys_patch, values_patch = (
        lax.all_to_all(spatial_out, "seq", split_axis=2, concat_axis=1, tiled=True),
        lax.all_to_all(temporal_keys, "seq", split_axis=2, concat_axis=1, tiled=True),
        lax.all_to_all(temporal_values, "seq", split_axis=2, concat_axis=1, tiled=True),
    )
    patch_dims = spatial_patch.shape
    spatial_rows = spatial_patch.reshape(-1, width)
    projected = (
        jnp.dot(spatial_rows, full_weight, preferred_element_type=jnp.float32)
        .astype(jnp.bfloat16)
        .reshape(patch_dims)
    )
    temporal_out, temporal_back = jax.vjp(temporal_block, projected, keys_patch, values_patch)
    d_projected, d_keys_patch, d_values_patch = temporal_back(out_grad)
    d_rows = d_projected.reshape(-1, width)
    d_spatial = lax.dot_general(
        d_rows, full_weight, (((1,), (1,)), ((), ())), preferred_element_type=jnp.float32
    ).astype(jnp.bfloat16)
    partial_rows = lax.psum_scatter(
        lax.dot_general(
            spatial_rows, d_rows, (((0,), (0,)), ((), ())), preferred_element_type=jnp.float32
        ).astype(jnp.bfloat16),
        "seq",
        scatter_dimension=0,
        tiled=True,
    )
    d_weight = lax.psum(partial_rows, "dp")
    d_spatial = d_spatial.reshape(patch_dims)
    d_spatial_frame, d_temporal_keys, d_temporal_values = (
        lax.all_to_all(d_spatial, "seq", split_axis=1, concat_axis=2, tiled=True),
        lax.all_to_all(d_keys_patch, "seq", split_axis=1, concat_axis=2, tiled=True),
        lax.all_to_all(d_values_patch, "seq", split_axis=1, concat_axis=2, tiled=True),
    )
    d_queries, d_keys, d_values = spatial_back(d_spatial_frame)
    return (d_queries, d_keys, d_values, d_temporal_keys, d_temporal_values, d_weight)


def solution(mesh):
    return jax.shard_map(
        per_device,
        mesh=mesh,
        in_specs=(
            P("dp", "seq", None, None),
            P("dp", "seq", None, None),
            P("dp", "seq", None, None),
            P("dp", "seq", None, None),
            P("dp", "seq", None, None),
            P("dp", "seq", None, None),
            P("seq", None),
            P("dp", None, "seq", None),
        ),
        out_specs=(
            P("dp", "seq", None, None),
            P("dp", "seq", None, None),
            P("dp", "seq", None, None),
            P("dp", "seq", None, None),
            P("dp", "seq", None, None),
            P("seq", None),
        ),
        check_vma=False,
    )
```

profile of v0, /device:TPU:1, one launch (start us, length us, event | category | flops | bytes accessed | tf_op | source)
XLA Modules:
  0.0 465.2 jit_solution(6171821005974624386)
XLA Ops:
  7.2 0.7 all-gather.2.cloned.1.call-update
  7.9 2.3 copy.316
  10.8 5.4 %reduce.9 = bf16[256,1536]{1,0:T(8,128)(2,1)S(1)} reduce(bf16[256,1,1,1536]{3,2,1,0:T(2,128)(2,1)S(1)} %bitcast.158, bf16[]{:T(256)} %broadcast.273), dimensions={1,2}, to_apply=%bitcast.142.reduce_sub_computation | reduce | bytes 1572866
  16.2 1.2 reshape.494
  17.4 12.7 %all-to-all-start.2 = ((bf16[32,2,6144]{2,1,0:T(2,128)(2,1)}), bf16[32,2,6144]{2,1,0:T(2,128)(2,1)}, u32[]{:S(2)}, u32[]{:S(2)}) async-start(bf16[32,2,6144]{2,1,0:T(2,128)(2,1)} %reshape.494), calls=%async_computation.2 | async-start | bytes 1572864 | tf_op jit(solution)/shard_map/all_to_all | solution.py:87
  30.5 2.0 copy.192
  32.5 4.1 copy.317
  36.6 7.3 %reduce.10 = bf16[256,1536]{1,0:T(8,128)(2,1)} reduce(bf16[256,1,1,1536]{3,2,1,0:T(2,128)(2,1)} %bitcast.161, bf16[]{:T(256)} %broadcast.273), dimensions={1,2}, to_apply=%bitcast.143.reduce_sub_computation | reduce | bytes 1572866
  43.9 3.1 reshape.498
  47.2 8.6 %all-to-all-done.2 = bf16[32,2,6144]{2,1,0:T(2,128)(2,1)} async-done(((bf16[32,2,6144]{2,1,0:T(2,128)(2,1)}), bf16[32,2,6144]{2,1,0:T(2,128)(2,1)}, u32[]{:S(2)}, u32[]{:S(2)}) %all-to-all-start.2) | async-done | bytes 786464 | tf_op jit(solution)/shard_map/all_to_all | solution.py:87
  55.8 6.3 %all-to-all-start = ((bf16[32,2,6144]{2,1,0:T(2,128)(2,1)}), bf16[32,2,6144]{2,1,0:T(2,128)(2,1)}, u32[]{:S(2)}, u32[]{:S(2)}) async-start(bf16[32,2,6144]{2,1,0:T(2,128)(2,1)} %reshape.498), calls=%async_computation | async-start | bytes 1572864 | tf_op jit(solution)/shard_map/all_to_all | solution.py:88
  62.3 1.2 copy.196
  63.5 2.8 fusion.9
  67.5 1.3 convolution_convert_fusion.6
  68.7 4.9 %copy.198 = bf16[1,1,256,1536]{3,1,0,2:T(2,128)(2,1)} copy(bf16[1,1,256,1536]{2,3,1,0:T(8,128)(2,1)} %bitcast.178) | data formatting | bytes 1572864 | tf_op jit(solution)/shard_map/jvp()/reshape | solution.py:81
  73.6 7.3 %reduce.8 = bf16[256,1536]{1,0:T(8,128)(2,1)} reduce(bf16[256,1,1,1536]{3,2,1,0:T(2,128)(2,1)} %bitcast.159, bf16[]{:T(256)} %broadcast.273), dimensions={1,2}, to_apply=%bitcast.120.reduce_sub_computation | reduce | bytes 1572866
  80.9 3.2 reshape.496
  84.1 2.9 all-to-all-done
  86.9 7.2 %all-to-all-start.1 = ((bf16[32,2,6144]{2,1,0:T(2,128)(2,1)}), bf16[32,2,6144]{2,1,0:T(2,128)(2,1)}, u32[]{:S(2)}, u32[]{:S(2)}) async-start(bf16[32,2,6144]{2,1,0:T(2,128)(2,1)} %reshape.496), calls=%async_computation.1 | async-start | bytes 1572864 | tf_op jit(solution)/shard_map/all_to_all | solution.py:86
  94.4 5.8 %reshape.495 = bf16[256,1,1,1536]{3,2,1,0:T(2,128)(2,1)} reshape(bf16[32,2,6144]{2,1,0:T(2,128)(2,1)} %all-to-all-done.2) | data formatting | bytes 1572864
  100.2 2.6 multiply_reduce_fusion
  102.8 1.1 copy.204
  104.6 5.8 %reshape.499 = bf16[256,1,1,1536]{3,2,1,0:T(2,128)(2,1)} reshape(bf16[32,2,6144]{2,1,0:T(2,128)(2,1)} %all-to-all-done) | data formatting | bytes 1572864
  110.4 2.4 copy.314
  112.8 9.9 %all-to-all-done.1 = bf16[32,2,6144]{2,1,0:T(2,128)(2,1)} async-done(((bf16[32,2,6144]{2,1,0:T(2,128)(2,1)}), bf16[32,2,6144]{2,1,0:T(2,128)(2,1)}, u32[]{:S(2)}, u32[]{:S(2)}) %all-to-all-start.1) | async-done | bytes 786464 | tf_op jit(solution)/shard_map/all_to_all | solution.py:86
  122.7 5.8 %reshape.497 = bf16[256,1,1,1536]{3,2,1,0:T(2,128)(2,1)} reshape(bf16[32,2,6144]{2,1,0:T(2,128)(2,1)} %all-to-all-done.1) | data formatting | bytes 1572864
  128.5 3.6 convert_bitcast_fusion
  132.1 6.1 %multiply_reduce_fusion.1 = (f32[32,8,12]{1,2,0:T(8,128)}, f32[256,1536]{1,0:T(8,128)}) fusion(bf16[1536,1536]{1,0:T(8,128)(2,1)} %all-gather.2.cloned.1.call-done, bf16[1,1,256,1536]{3,1,0,2:T(2,128)(2,1)} %bitcast.166), kind=kOutput, calls=%fused_computation.56 | convolution fusion | flops 1209529344 | bytes 7090176 | tf_op jit(solution)/shard_map/dot_general | solution.py:93
  138.2 1.1 copy.199
  139.9 4.3 fusion.64
  144.3 1.2 fusion.14
  146.3 0.8 copy-done.14
  147.1 2.5 fusion.26
  149.6 1.5 fusion.15
  151.1 0.9 copy-done.16
  152.0 3.8 convolution_convert_fusion
  155.8 5.0 %fusion.8 = bf16[1,32,8,1536]{3,2,0,1:T(8,128)(2,1)} fusion(bf16[1536,1536]{1,0:T(8,128)(2,1)} %all-gather.2.cloned.1.call-done, bf16[1,32,8,12,128]{4,1,3,2,0:T(8,128)(2,1)} %copy-done.16), kind=kOutput, calls=%fused_computation.15 | convolution fusion | flops 1208352768 | bytes 6291456 | tf_op jit(solution)/shard_map/dot_general | solution.py:100
  160.8 6.1 %all-to-all-start.3 = ((bf16[1,32,8,1536]{3,2,0,1:T(8,128)(2,1)}), bf16[1,32,8,1536]{3,2,0,1:T(8,128)(2,1)}, u32[]{:S(2)}, u32[]{:S(2)}) async-start(bf16[1,32,8,1536]{3,2,0,1:T(8,128)(2,1)} %fusion.8), calls=%async_computation.3 | async-start | bytes 1572864 | tf_op jit(solution)/shard_map/all_to_all | solution.py:114
  167.6 2.4 fusion.29
  170.0 1.4 copy.312
  171.5 3.5 fusion.21
  175.0 16.1 %all-to-all-done.3 = bf16[1,32,8,1536]{3,2,0,1:T(8,128)(2,1)} async-done(((bf16[1,32,8,1536]{3,2,0,1:T(8,128)(2,1)}), bf16[1,32,8,1536]{3,2,0,1:T(8,128)(2,1)}, u32[]{:S(2)}, u32[]{:S(2)}) %all-to-all-start.3) | async-done | bytes 786464 | tf_op jit(solution)/shard_map/all_to_all | solution.py:114
  191.1 6.6 %all-to-all-start.5 = ((bf16[1,32,8,1536]{3,2,0,1:T(8,128)(2,1)}), bf16[1,32,8,1536]{3,2,0,1:T(8,128)(2,1)}, u32[]{:S(2)}, u32[]{:S(2)}) async-start(bf16[1,32,8,1536]{3,2,0,1:T(8,128)(2,1)} %bitcast.174), calls=%async_computation.5 | async-start | bytes 1572864 | tf_op jit(solution)/shard_map/all_to_all | solution.py:116
  197.8 0.9 fusion.53
  198.7 2.3 fusion.18
  201.0 1.4 copy.313
  202.4 2.4 reshape.482
  204.8 2.5 copy.215
  207.3 2.6 fusion.5
  209.9 1.2 copy-done.20
  211.0 2.3 fusion.22
  213.4 8.3 %all-to-all-done.5 = bf16[1,32,8,1536]{3,2,0,1:T(8,128)(2,1)} async-done(((bf16[1,32,8,1536]{3,2,0,1:T(8,128)(2,1)}), bf16[1,32,8,1536]{3,2,0,1:T(8,128)(2,1)}, u32[]{:S(2)}, u32[]{:S(2)}) %all-to-all-start.5) | async-done | bytes 786464 | tf_op jit(solution)/shard_map/all_to_all | solution.py:116
  221.6 7.1 %all-to-all-start.4 = ((bf16[1,32,8,1536]{3,2,0,1:T(8,128)(2,1)}), bf16[1,32,8,1536]{3,2,0,1:T(8,128)(2,1)}, u32[]{:S(2)}, u32[]{:S(2)}) async-start(bf16[1,32,8,1536]{3,2,0,1:T(8,128)(2,1)} %bitcast.173), calls=%async_computation.4 | async-start | bytes 1572864 | tf_op jit(solution)/shard_map/all_to_all | solution.py:115
  229.1 3.7 fusion.23
  233.0 1.2 fusion.16
  234.8 1.2 fusion.17
  236.0 150.9 %reduce-scatter.2.cloned.1.call-done = bf16[48,1536]{1,0:T(8,128)(2,1)} async-done(((bf16[1536,1536]{1,0:T(8,128)(2,1)}), bf16[48,1536]{1,0:T(8,128)(2,1)}) %reduce-scatter.2.cloned.1.call-update) | async-done | bytes 147472 | tf_op jit(solution)/shard_map/reduce_scatter | solution.py:103
  387.0 1.8 convolution_convert_fusion.9
  388.8 1.2 copy.231
  389.9 1.2 copy.229
  391.1 1.2 copy.230
  392.3 61.0 %all-reduce.2.cloned.1.call-done = bf16[48,1536]{1,0:T(8,128)(2,1)} async-done(((bf16[48,1536]{1,0:T(8,128)(2,1)}), bf16[48,1536]{1,0:T(8,128)(2,1)}) %all-reduce.2.cloned.1.call-update) | async-done | bytes 147472 | tf_op jit(solution)/shard_map/psum | solution.py:111
  453.3 2.1 copy.321
  455.4 2.1 copy.322
  (121 shorter events, 7.3 us)
Async XLA Ops:
  7.2 125.0 %all-gather.2.cloned.1.call-start = ((), (), s32[]{:S(2)}) async-start(), calls=%async_computation.7 | async-start | bytes 4866048 | tf_op jit(solution)/shard_map/all_gather | solution.py:84
  16.2 13.9 %copy-start.45 = (s32[1,1,2,2]{3,2,1,0:T(2,128)S(1)}, s32[1,1,2,2]{3,2,1,0:T(2,128)}, u32[]{:S(2)}) copy-start(s32[1,1,2,2]{3,2,1,0:T(2,128)} %param.13) | copy-start | bytes 52
  16.2 14.0 %copy-start.22 = (bf16[1,1,256,1536]{3,2,1,0:T(8,128)(2,1)S(1)}, bf16[1,1,256,1536]{3,2,1,0:T(8,128)(2,1)}, u32[]{:S(2)}) copy-start(bf16[1,1,256,1536]{3,2,1,0:T(8,128)(2,1)} %param.8) | copy-start | bytes 2359300
  17.4 38.4 %all-to-all-start.2 = ((bf16[32,2,6144]{2,1,0:T(2,128)(2,1)}), bf16[32,2,6144]{2,1,0:T(2,128)(2,1)}, u32[]{:S(2)}, u32[]{:S(2)}) async-start(bf16[32,2,6144]{2,1,0:T(2,128)(2,1)} %reshape.494), calls=%async_computation.2 | async-start | bytes 1572864 | tf_op jit(solution)/shard_map/all_to_all | solution.py:87
  30.5 16.6 %copy-start.3 = (f32[1,1,256,1536]{2,3,1,0:T(8,128)}, f32[1,1,256,1536]{2,3,1,0:T(8,128)S(1)}, u32[]{:S(2)}) copy-start(f32[1,1,256,1536]{2,3,1,0:T(8,128)S(1)} %copy.191) | copy-start | bytes 4718596
  32.5 29.7 %copy-start = (f32[1,1,256,1536]{2,3,1,0:T(8,128)}, f32[1,1,256,1536]{2,3,1,0:T(8,128)S(1)}, u32[]{:S(2)}) copy-start(f32[1,1,256,1536]{2,3,1,0:T(8,128)S(1)} %copy.192) | copy-start | bytes 4718596
  47.1 16.3 %copy-start.37 = (f32[256,12]{0,1:T(8,128)}, f32[256,12]{0,1:T(8,128)S(1)}, u32[]{:S(2)}) copy-start(f32[256,12]{0,1:T(8,128)S(1)} %multiply_reduce_fusion.3) | copy-start | bytes 36868
  47.2 15.1 %copy-start.21 = (bf16[1,1,256,1536]{3,2,1,0:T(8,128)(2,1)S(1)}, bf16[1,1,256,1536]{3,2,1,0:T(8,128)(2,1)}, u32[]{:S(2)}) copy-start(bf16[1,1,256,1536]{3,2,1,0:T(8,128)(2,1)} %param.10) | copy-start | bytes 2359300
  55.8 31.1 %all-to-all-start = ((bf16[32,2,6144]{2,1,0:T(2,128)(2,1)}), bf16[32,2,6144]{2,1,0:T(2,128)(2,1)}, u32[]{:S(2)}, u32[]{:S(2)}) async-start(bf16[32,2,6144]{2,1,0:T(2,128)(2,1)} %reshape.498), calls=%async_computation | async-start | bytes 1572864 | tf_op jit(solution)/shard_map/all_to_all | solution.py:88
  62.3 1.2 copy-start.39
  63.5 2.8 copy-start.33
  63.5 2.8 copy-start.35
  66.3 1.1 copy-start.8
  66.9 1.8 copy-start.6
  86.9 35.8 %all-to-all-start.1 = ((bf16[32,2,6144]{2,1,0:T(2,128)(2,1)}), bf16[32,2,6144]{2,1,0:T(2,128)(2,1)}, u32[]{:S(2)}, u32[]{:S(2)}) async-start(bf16[32,2,6144]{2,1,0:T(2,128)(2,1)} %reshape.496), calls=%async_computation.1 | async-start | bytes 1572864 | tf_op jit(solution)/shard_map/all_to_all | solution.py:86
  94.2 292.8 %reduce-scatter.2.cloned.1.call-start = ((), (), s32[]{:S(2)}) async-start(), calls=%async_computation.8 | async-start | bytes 4866048 | tf_op jit(solution)/shard_map/reduce_scatter | solution.py:103
  103.9 0.6 copy-start.27
  139.3 0.6 copy-start.29
  139.9 4.4 copy-start.19
  139.9 4.4 copy-start.24
  144.3 1.4 copy-start.12
  144.3 1.4 copy-start.31
  144.3 1.9 copy-start.10
  144.3 2.7 copy-start.14
  145.6 4.0 copy-start.25
  145.6 3.9 copy-start.43
  147.0 2.5 copy-start.30
  149.6 2.4 copy-start.15
  151.1 0.9 copy-start.16
  160.8 30.3 %all-to-all-start.3 = ((bf16[1,32,8,1536]{3,2,0,1:T(8,128)(2,1)}), bf16[1,32,8,1536]{3,2,0,1:T(8,128)(2,1)}, u32[]{:S(2)}, u32[]{:S(2)}) async-start(bf16[1,32,8,1536]{3,2,0,1:T(8,128)(2,1)} %fusion.8), calls=%async_computation.3 | async-start | bytes 1572864 | tf_op jit(solution)/shard_map/all_to_all | solution.py:114
  167.6 3.9 copy-start.11
  167.6 3.9 copy-start.13
  167.6 3.9 copy-start.26
  167.6 3.9 copy-start.32
  167.6 3.9 copy-start.44
  170.0 1.5 copy-start.9
  175.0 22.8 %copy-start.28 = (f32[32,8,12]{0,1,2:T(8,128)S(1)}, f32[32,8,12]{0,1,2:T(8,128)}, u32[]{:S(2)}) copy-start(f32[32,8,12]{0,1,2:T(8,128)} %copy-done.27) | copy-start | bytes 36868
  191.1 30.5 %all-to-all-start.5 = ((bf16[1,32,8,1536]{3,2,0,1:T(8,128)(2,1)}), bf16[1,32,8,1536]{3,2,0,1:T(8,128)(2,1)}, u32[]{:S(2)}, u32[]{:S(2)}) async-start(bf16[1,32,8,1536]{3,2,0,1:T(8,128)(2,1)} %bitcast.174), calls=%async_computation.5 | async-start | bytes 1572864 | tf_op jit(solution)/shard_map/all_to_all | solution.py:116
  202.4 4.9 %copy-start.42 = (f32[12,256]{1,0:T(8,128)S(1)}, f32[12,256]{1,0:T(8,128)}, u32[]{:S(2)}) copy-start(f32[12,256]{1,0:T(8,128)} %multiply_divide_fusion.1) | copy-start | bytes 36868
  207.3 3.8 copy-start.1
  207.3 3.8 copy-start.4
  207.3 3.8 copy-start.36
  209.9 1.2 copy-start.20
  213.4 15.8 %copy-start.34 = (f32[256,12]{0,1:T(8,128)S(1)}, f32[256,12]{0,1:T(8,128)}, u32[]{:S(2)}) copy-start(f32[256,12]{0,1:T(8,128)} %copy-done.33) | copy-start | bytes 36868
  221.6 167.2 %all-to-all-start.4 = ((bf16[1,32,8,1536]{3,2,0,1:T(8,128)(2,1)}), bf16[1,32,8,1536]{3,2,0,1:T(8,128)(2,1)}, u32[]{:S(2)}, u32[]{:S(2)}) async-start(bf16[1,32,8,1536]{3,2,0,1:T(8,128)(2,1)} %bitcast.173), calls=%async_computation.4 | async-start | bytes 1572864 | tf_op jit(solution)/shard_map/all_to_all | solution.py:115
  228.7 4.1 copy-start.38
  228.8 4.1 copy-start.40
  228.8 224.5 %all-reduce.2.cloned.1.call-start = ((), (), s32[]{:S(2)}) async-start(), calls=%async_computation.9 | async-start | bytes 294912 | tf_op jit(solution)/shard_map/psum | solution.py:111
  229.1 3.8 copy-start.5
  232.9 1.7 copy-start.2
  232.9 1.9 copy-start.23
  234.8 152.1 %copy-start.7 = (bf16[12,256,256]{1,2,0:T(8,128)(2,1)S(1)}, bf16[12,256,256]{1,2,0:T(8,128)(2,1)}, u32[]{:S(2)}) copy-start(bf16[12,256,256]{1,2,0:T(8,128)(2,1)} %copy-done.6) | copy-start | bytes 4718596
  388.8 1.2 copy-start.17
  388.8 2.3 copy-start.18
  453.3 4.2 copy-start.41
Sparse Core Ops, SparseCore 0:
  10.6 108.2 all-gather.1
  155.9 230.9 reduce-scatter.1
  389.3 63.9 all-reduce.1
where the time goes:
time: 474 us; the launch traced here: 465 us
  waiting for transfers between devices  258 us (54%)
  local copies, waits for them, and re-layouts  67 us (14%)
  starting transfers between devices  46.7 us (10%)
  matrix products  43.1 us (9%)
  other arithmetic  34.9 us (7%)
  between operations  15 us (3%)
    reduce_scatter x1, waiting for transfers between devices, per_device(): lax.psum_scatter(lax.dot_general(spatial_rows, d_rows, (((0,), (0,)), (()...  151 us
    psum x1, waiting for transfers between devices, per_device(): d_weight = lax.psum(partial_rows, 'dp')  61 us
    unnamed x110, local copies, waits for them, and re-layouts  47.5 us
    unnamed x3, other arithmetic  20 us
    all_to_all x1, waiting for transfers between devices, per_device(): lax.all_to_all(d_spatial, 'seq', split_axis=1, concat_axis=2, tiled=True)  16.1 us
    all_to_all x1, starting transfers between devices, per_device(): lax.all_to_all(temporal_keys, 'seq', split_axis=2, concat_axis=1, tiled=T...  12.7 us
    dot_general x3, matrix products, temporal_block(): jnp.einsum('cfphd,cgphd->cphfg', query_norm, key_norm, preferred_element_...  10.2 us
    all_to_all x1, waiting for transfers between devices, per_device(): lax.all_to_all(spatial_out, 'seq', split_axis=2, concat_axis=1, tiled=True)  9.94 us
  transfers between devices with their start and end apart: 9, of which 7 were waited for; matrix products, arithmetic and copies ran while one was open for 24% of the time, Pallas kernels for 0%

commit v1 on v0

v1 whole, which is shorter than its diff:
```python
import math

import jax
import jax.numpy as jnp
from jax import lax
from jax.experimental import pallas as pl
from jax.experimental.pallas import tpu as pltpu
from jax.sharding import PartitionSpec as P

HEADS = 12
HEAD_DIM = 128
TILE = 128
WIDTH = HEADS * HEAD_DIM
NX, NY, NZ = 4, 4, 8
SEQ = NZ * NY
ROWS = 48
PATCH = 256
PAIR = 2 * HEAD_DIM
PAIRS = WIDTH // PAIR
CHUNK = 512
THIRDS = WIDTH // CHUNK
COLS = WIDTH // NX
SCALE = 1.0 / math.sqrt(HEAD_DIM)
SCALE2 = SCALE * math.log2(math.e)
EPS = 1e-06
MESH = pl.DeviceIdType.MESH
F32 = jnp.float32
BF16 = jnp.bfloat16


def dot(a, b, contract):
    return lax.dot_general(a, b, ((contract[:1], contract[1:]), ((), ())), preferred_element_type=F32)


def inverse_rms(a):
    return lax.rsqrt(jnp.mean(a * a, axis=-1, keepdims=True) + EPS)


def norm_back(grad, normed, inverse):
    return (inverse * SCALE) * (grad - normed * jnp.mean(grad * normed, axis=-1, keepdims=True))


def softmax(q_norm, k_norm, mask):
    exps = jnp.exp2(dot(q_norm, k_norm, (1, 1)) * SCALE2) * mask
    return exps * (1.0 / jnp.sum(exps, axis=-1, keepdims=True))


def attention_back(weights, weights_b, q, k, qn, kn, rq, rk, qn_b, kn_b, v, grad):
    d_weights = dot(grad, v, (1, 1))
    delta = jnp.sum(weights * d_weights, axis=-1, keepdims=True)
    d_scores = (weights * (d_weights - delta)).astype(BF16)
    d_v = dot(weights_b, grad, (0, 0))
    d_q = norm_back(dot(d_scores, kn_b, (1, 0)), qn, rq)
    d_k = norm_back(dot(d_scores, qn_b, (0, 0)), kn, rk)
    return d_q, d_k, d_v


def wait_for(ref, sem):
    pltpu.make_async_copy(ref, ref, sem).wait()


def kernel(
    tile_ref, q_ref, k_ref, v_ref, tk_ref, tv_ref, w_ref, og_ref,
    dq_ref, dk_ref, dv_ref, dtk_ref, dtv_ref, dw_ref,
    weight, mask, tmask, spatial, k_buf, v_buf, s_buf, s_mat, d_mat, attn,
    dk_send, dv_send, ds_send, ds_buf,
    part, core_in, x_in, x_sum, y_in, y_sum, z_in, final,
    send, a2a_in, w_in, wx_in, core_sem, x_sem, y_sem, z_sem, out_sem, g_send, local,
):
    d = lax.axis_index("dp")
    s = lax.axis_index("seq")
    x, c = d // 2, d % 2
    z, y = s // NY, s % NY
    sibling = {"dp": x * 2 + 1 - c}
    active = y % 2 == c
    idle = y % 2 != c

    def seq_peer(o):
        return lax.rem(s + o, SEQ)

    def x_peer(o):
        return {"dp": lax.rem(x + o, NX) * 2 + c}

    def y_peer(o):
        return {"seq": z * NY + lax.rem(y + o, NY)}

    def z_peer(o):
        return {"seq": lax.rem(z + o, NZ) * NY + y}

    def remote(src, dst, send_sem, recv_sem, device):
        pltpu.make_async_remote_copy(
            src, dst, send_sem, recv_sem, device_id=device, device_id_type=MESH
        ).start()

    def exchange(src, dst, lanes, send_sem, recv_sem):
        pltpu.make_async_copy(src.at[s, :, lanes], dst.at[s, :, lanes], recv_sem).start()

        @pl.loop(1, SEQ)
        def _(o):
            j = seq_peer(o)
            remote(src.at[j, :, lanes], dst.at[s, :, lanes], send_sem, recv_sem, {"seq": j})

    def lanes_of(n, width):
        return pl.ds(pl.multiple_of(n * width, width), width)

    all_lanes = pl.ds(0, WIDTH)
    own_cols = lanes_of(x, COLS)

    weight[z, y] = w_ref[...]

    barrier = pltpu.get_barrier_semaphore()

    @pl.loop(1, SEQ)
    def _(o):
        pl.semaphore_signal(barrier, inc=1, device_id={"seq": seq_peer(o)}, device_id_type=MESH)

    @pl.loop(1, 2 * NX)
    def _(o):
        pl.semaphore_signal(barrier, inc=1, device_id={"dp": lax.rem(d + o, 2 * NX)}, device_id_type=MESH)

    pl.semaphore_wait(barrier, SEQ - 1 + 2 * NX - 1)

    @pl.when(active)
    def _():
        src = weight.at[z, y, :, own_cols]

        @pl.loop(1, NZ)
        def _(o):
            remote(src, src, send.at[0], w_in.at[0], z_peer(o))

    exchange(tk_ref, k_buf, all_lanes, send.at[1], a2a_in.at[0])

    ones = jnp.ones((TILE, TILE), F32)
    for a in range(2):
        for b in range(2):
            value = 1.0 if a == b else jnp.where(tile_ref[a, b] == 1, 1.0, 0.0).astype(F32)
            mask[a * TILE:(a + 1) * TILE, b * TILE:(b + 1) * TILE] = ones * value
    row = lax.broadcasted_iota(jnp.int32, (PATCH, PATCH), 0)
    col = lax.broadcasted_iota(jnp.int32, (PATCH, PATCH), 1)
    tmask[...] = jnp.where(row % 8 == col % 8, 1.0, 0.0).astype(F32)

    @pl.loop(0, PAIRS)
    def _(n):
        lanes = lanes_of(n, PAIR)
        q2, k2 = q_ref[:, lanes].astype(F32), k_ref[:, lanes].astype(F32)
        v2 = v_ref[:, lanes]
        outs = []
        for h in range(2):
            cut = slice(h * HEAD_DIM, (h + 1) * HEAD_DIM)
            q, k = q2[:, cut], k2[:, cut]
            qn = (q * inverse_rms(q)).astype(BF16)
            kn = (k * inverse_rms(k)).astype(BF16)
            weights = softmax(qn, kn, mask[...]).astype(BF16)
            attn[2 * n + h] = weights
            outs.append(dot(weights, v2[:, cut], (1, 0)))
        out = jnp.concatenate(outs, axis=1)
        spatial[:, :, lanes] = out.reshape(SEQ, 8, PAIR).astype(BF16)

        @pl.when(n % 2 == 1)
        def _():
            exchange(spatial, s_buf, lanes_of(n // 2, CHUNK), send.at[2], a2a_in.at[1])

        @pl.when(n == 1)
        def _():
            @pl.when(active)
            def _():
                wait_for(weight.at[pl.ds(0, NZ - 1), y, :, own_cols], w_in.at[0])
                src = weight.at[:, y, :, own_cols]

                @pl.loop(1, NY)
                def _(o):
                    remote(src, src, send.at[3], w_in.at[1], y_peer(o))

        @pl.when(n == 4)
        def _():
            @pl.when(active)
            def _():
                wait_for(weight.at[:, 0, :, own_cols], w_in.at[1])

            @pl.when(idle)
            def _():
                wait_for(weight.at[:, pl.ds(0, 2), :, own_cols], w_in.at[1])

            for h in range(2):
                src = weight.at[:, c + 2 * h, :, own_cols]

                @pl.loop(1, NX)
                def _(o):
                    remote(src, src, send.at[4], wx_in.at[o - 1], x_peer(o))

                remote(src, src, send.at[5], w_in.at[2], sibling)

    exchange(tv_ref, v_buf, all_lanes, send.at[6], a2a_in.at[2])

    for o in (1, 3, 2):
        cols = lanes_of(lax.rem(x + NX - o, NX), COLS)
        wait_for(weight.at[:, pl.ds(0, 2), :, cols], wx_in.at[o - 1])
        for h in range(2):
            src = weight.at[:, c + 2 * h, :, cols]
            remote(src, src, send.at[5], w_in.at[2], sibling)

    wait_for(s_buf, a2a_in.at[1])
    for n in range(PAIRS):
        lanes = slice(n * PAIR, (n + 1) * PAIR)
        s_mat[:, lanes] = s_buf[:, :, lanes].astype(F32).reshape(PATCH, PAIR).astype(BF16)
    wait_for(weight.at[:, pl.ds(0, 2)], w_in.at[2])
    wait_for(k_buf, a2a_in.at[0])
    wait_for(v_buf, a2a_in.at[2])

    @pl.loop(0, PAIRS)
    def _(n):
        lanes = lanes_of(n, PAIR)
        rows = weight[:, :, :, lanes].reshape(WIDTH, PAIR)
        q2 = dot(s_mat[...], rows, (1, 0)).astype(BF16).astype(F32)
        k2 = k_buf[:, :, lanes].astype(F32).reshape(PATCH, PAIR)
        v2 = v_buf[:, :, lanes].astype(F32).reshape(PATCH, PAIR).astype(BF16)
        g2 = og_ref[:, :, lanes].astype(F32).reshape(PATCH, PAIR).astype(BF16)
        d_qs, d_ks, d_vs = [], [], []
        for h in range(2):
            cut = slice(h * HEAD_DIM, (h + 1) * HEAD_DIM)
            q, k = q2[:, cut], k2[:, cut]
            rq, rk = inverse_rms(q), inverse_rms(k)
            qn, kn = q * rq, k * rk
            qn_b, kn_b = qn.astype(BF16), kn.astype(BF16)
            weights = softmax(qn_b, kn_b, tmask[...])
            d_q, d_k, d_v = attention_back(
                weights, weights.astype(BF16), q, k, qn, kn, rq, rk, qn_b, kn_b, v2[:, cut], g2[:, cut]
            )
            d_qs.append(d_q)
            d_ks.append(d_k)
            d_vs.append(d_v)
        d_mat[:, lanes] = jnp.concatenate(d_qs, axis=1).astype(BF16)
        dk_send[:, :, lanes] = jnp.concatenate(d_ks, axis=1).reshape(SEQ, 8, PAIR).astype(BF16)
        dv_send[:, :, lanes] = jnp.concatenate(d_vs, axis=1).reshape(SEQ, 8, PAIR).astype(BF16)

        @pl.when(n == 1)
        def _():
            first = pl.ds(0, CHUNK)
            exchange(dk_send, dtk_ref, first, send.at[7], a2a_in.at[3])
            exchange(dv_send, dtv_ref, first, send.at[8], a2a_in.at[4])

    @pl.loop(0, NZ // 2)
    def _(m):
        rows = weight[pl.ds(2 * m, 2)].reshape(2 * NY * ROWS, WIDTH)
        out = dot(d_mat[...], rows, (1, 1))
        lanes = lanes_of(m, 2 * NY * ROWS)
        ds_send[:, :, lanes] = out.reshape(SEQ, 8, 2 * NY * ROWS).astype(BF16)
        exchange(ds_send, ds_buf, lanes, send.at[9], a2a_in.at[5])

    rest = pl.ds(CHUNK, WIDTH - CHUNK)
    exchange(dk_send, dtk_ref, rest, send.at[7], a2a_in.at[3])
    exchange(dv_send, dtv_ref, rest, send.at[8], a2a_in.at[4])

    @pl.loop(0, THIRDS)
    def _(g):
        cols = d_mat[:, lanes_of(g, CHUNK)]

        @pl.loop(0, NZ // 2)
        def _(m):
            block = dot(s_mat[:, lanes_of(m, 2 * NY * ROWS)], cols, (0, 0))
            part[g, pl.ds(2 * m, 2)] = block.reshape(2, NY, ROWS, CHUNK).astype(BF16)

        for h in range(2):
            remote(part.at[g, :, 1 - c + 2 * h], core_in.at[g, h], g_send.at[0], core_sem.at[g], sibling)

    def x_step(g):
        wait_for(core_in.at[g], core_sem.at[g])
        for h in range(2):
            own = part[g, :, c + 2 * h].astype(F32) + core_in[g, h].astype(F32)
            part[g, :, c + 2 * h] = own.astype(BF16)

            @pl.loop(1, NX)
            def _(o):
                to = lax.rem(x + o, NX)
                remote(
                    part.at[g, :, c + 2 * h, :, lanes_of(to, HEAD_DIM)], x_in.at[g, o - 1, h],
                    g_send.at[1], x_sem.at[g], x_peer(o),
                )

    def y_step(g):
        wait_for(x_in.at[g], x_sem.at[g])
        for h in range(2):
            total = part[g, :, c + 2 * h, :, lanes_of(x, HEAD_DIM)].astype(F32)
            for o in range(NX - 1):
                total = total + x_in[g, o, h].astype(F32)
            x_sum[g, h] = total.astype(BF16)
            owner = c + 2 * h

            @pl.when(y != owner)
            def _():
                away = lax.rem(y - owner + NY, NY)
                remote(x_sum.at[g, h], y_in.at[g, away - 1], g_send.at[2], y_sem.at[g], {"seq": z * NY + owner})

    def z_step(g):
        @pl.when(active)
        def _():
            wait_for(y_in.at[g], y_sem.at[g])
            total = x_sum[g, y // 2].astype(F32)
            for o in range(NY - 1):
                total = total + y_in[g, o].astype(F32)
            y_sum[g] = total.astype(BF16)

            @pl.loop(1, NZ)
            def _(o):
                remote(
                    y_sum.at[g, lax.rem(z + o, NZ)], z_in.at[g, o - 1], g_send.at[3], z_sem.at[g], z_peer(o)
                )

    def out_step(g):
        @pl.when(active)
        def _():
            wait_for(z_in.at[g], z_sem.at[g])
            total = y_sum[g, z].astype(F32)
            for o in range(NZ - 1):
                total = total + z_in[g, o].astype(F32)
            final[g] = total.astype(BF16)
            dst = dw_ref.at[:, pl.ds(pl.multiple_of(g * CHUNK + x * HEAD_DIM, HEAD_DIM), HEAD_DIM)]
            pltpu.make_async_copy(final.at[g], dst, out_sem).start()

            @pl.loop(1, 2 * NX)
            def _(o):
                remote(final.at[g], dst, g_send.at[4], out_sem, {"dp": lax.rem(d + o, 2 * NX)})

    for g in range(THIRDS):
        x_step(g)
    y_step(0)
    y_step(1)

    wait_for(ds_buf, a2a_in.at[5])

    @pl.loop(0, PAIRS)
    def _(n):
        lanes = lanes_of(n, PAIR)
        q2, k2 = q_ref[:, lanes].astype(F32), k_ref[:, lanes].astype(F32)
        v2 = v_ref[:, lanes]
        g2 = ds_buf[:, :, lanes].astype(F32).reshape(PATCH, PAIR).astype(BF16)
        d_qs, d_ks, d_vs = [], [], []
        for h in range(2):
            cut = slice(h * HEAD_DIM, (h + 1) * HEAD_DIM)
            q, k = q2[:, cut], k2[:, cut]
            rq, rk = inverse_rms(q), inverse_rms(k)
            qn, kn = q * rq, k * rk
            weights = attn[2 * n + h]
            d_q, d_k, d_v = attention_back(
                weights.astype(F32), weights, q, k, qn, kn, rq, rk, qn.astype(BF16), kn.astype(BF16),
                v2[:, cut], g2[:, cut],
            )
            d_qs.append(d_q)
            d_ks.append(d_k)
            d_vs.append(d_v)
        dq_ref[:, lanes] = jnp.concatenate(d_qs, axis=1).astype(BF16)
        dk_ref[:, lanes] = jnp.concatenate(d_ks, axis=1).astype(BF16)
        dv_ref[:, lanes] = jnp.concatenate(d_vs, axis=1).astype(BF16)

        @pl.when(n == 1)
        def _():
            z_step(0)
            z_step(1)
            y_step(2)

        @pl.when(n == 4)
        def _():
            out_step(0)
            out_step(1)
            z_step(2)

    out_step(2)

    wait_for(dtk_ref, a2a_in.at[3])
    wait_for(dtv_ref, a2a_in.at[4])

    @pl.when(active)
    def _():
        wait_for(dw_ref, out_sem)

    @pl.when(idle)
    def _():
        wait_for(dw_ref, out_sem)

    sent = pl.ds(0, SEQ - 1)
    for i, buf in ((1, k_buf), (2, s_buf), (6, v_buf), (7, k_buf), (8, v_buf), (9, ds_buf)):
        wait_for(buf.at[sent], send.at[i])
    wait_for(weight.at[:, pl.ds(0, 2), :, pl.ds(0, 3 * COLS)], send.at[4])
    wait_for(weight.at[:, pl.ds(0, 2)], send.at[5])
    wait_for(core_in, g_send.at[0])
    wait_for(x_in, g_send.at[1])

    @pl.when(active)
    def _():
        wait_for(weight.at[pl.ds(0, NZ - 1), y, :, own_cols], send.at[0])
        wait_for(weight.at[:, 0, :, pl.ds(0, 3 * COLS)], send.at[3])
        wait_for(x_sum.at[:, 0], g_send.at[2])
        wait_for(z_in, g_send.at[3])
        wait_for(z_in, g_send.at[4])

    @pl.when(idle)
    def _():
        wait_for(x_sum, g_send.at[2])


def per_device(
    queries, keys_spatial, values_spatial, temporal_keys, temporal_values, tile_mask, query_weight, out_grad
):
    frame = (PATCH, WIDTH)
    blocks = (SEQ, 8, WIDTH)
    vmem = pl.BlockSpec(memory_space=pltpu.VMEM)
    smem = pl.BlockSpec(memory_space=pltpu.SMEM)
    anywhere = pl.BlockSpec(memory_space=pl.ANY)
    dma = pltpu.SemaphoreType.DMA

    def buf(*shape, kind=BF16):
        return pltpu.VMEM(shape, kind)

    d_q, d_k, d_v, d_tk, d_tv, d_w = pl.pallas_call(
        kernel,
        out_shape=(
            *(jax.ShapeDtypeStruct(frame, BF16) for _ in range(3)),
            *(jax.ShapeDtypeStruct(blocks, BF16) for _ in range(2)),
            jax.ShapeDtypeStruct((ROWS, WIDTH), BF16),
        ),
        in_specs=[smem, vmem, vmem, vmem, anywhere, anywhere, vmem, vmem],
        out_specs=(vmem, vmem, vmem, anywhere, anywhere, anywhere),
        scratch_shapes=[
            buf(NZ, NY, ROWS, WIDTH),
            buf(PATCH, PATCH, kind=F32),
            buf(PATCH, PATCH, kind=F32),
            buf(*blocks), buf(*blocks), buf(*blocks), buf(*blocks),
            buf(*frame), buf(*frame),
            buf(HEADS, PATCH, PATCH),
            buf(*blocks), buf(*blocks), buf(*blocks), buf(*blocks),
            buf(THIRDS, NZ, NY, ROWS, CHUNK),
            buf(THIRDS, 2, NZ, ROWS, CHUNK),
            buf(THIRDS, NX - 1, 2, NZ, ROWS, HEAD_DIM),
            buf(THIRDS, 2, NZ, ROWS, HEAD_DIM),
            buf(THIRDS, NY - 1, NZ, ROWS, HEAD_DIM),
            buf(THIRDS, NZ, ROWS, HEAD_DIM),
            buf(THIRDS, NZ - 1, ROWS, HEAD_DIM),
            buf(THIRDS, ROWS, HEAD_DIM),
            dma((10,)), dma((6,)), dma((3,)), dma((NX - 1,)),
            dma((THIRDS,)), dma((THIRDS,)), dma((THIRDS,)), dma((THIRDS,)), dma, dma((5,)), dma,
        ],
        compiler_params=pltpu.CompilerParams(
            collective_id=0, has_side_effects=True, vmem_limit_bytes=58 << 20
        ),
    )(
        tile_mask.reshape(2, 2),
        queries.reshape(frame),
        keys_spatial.reshape(frame),
        values_spatial.reshape(frame),
        temporal_keys.reshape(blocks),
        temporal_values.reshape(blocks),
        query_weight,
        out_grad.reshape(blocks),
    )
    whole = (1, 1, PATCH, WIDTH)
    return (*(a.reshape(whole) for a in (d_q, d_k, d_v, d_tk, d_tv)), d_w)


def solution(mesh):
    framed = P("dp", "seq", None, None)
    return jax.shard_map(
        per_device,
        mesh=mesh,
        in_specs=(framed,) * 6 + (P("seq", None), P("dp", None, "seq", None)),
        out_specs=(framed,) * 5 + (P("seq", None),),
        check_vma=False,
    )
```

time: 474 us -> 149 us (0.31); the launches traced: 465 us -> 149 us
  waiting for transfers between devices: 258 us -> 0 us
  Pallas kernels: 0 us -> 140 us
  local copies, waits for them, and re-layouts: 67 us -> 8.08 us
  starting transfers between devices: 46.7 us -> 0 us
  matrix products: 43.1 us -> 0 us
  other arithmetic: 34.9 us -> 0 us
  between operations: 15 us -> 0.66 us
    reduce_scatter x1 -> x0, waiting for transfers between devices: 151 us -> none  [per_device(): lax.psum_scatter(lax.dot_general(spatial_rows, d_rows, (((0,), (0,)), (()...]
    pallas_call x0 -> x1, Pallas kernels: none -> 140 us  [per_device(): pl.pallas_call(kernel, out_shape=(*(jax.ShapeDtypeStruct(frame, BF16) for...]
    psum x1 -> x0, waiting for transfers between devices: 61 us -> none  [per_device(): d_weight = lax.psum(partial_rows, 'dp')]
    all_to_all x6 -> x0, starting transfers between devices: 46.1 us -> none  [the longest x1 12.7 us: per_device(): lax.all_to_all(temporal_keys, 'seq', split_axis=2, concat_axis=1, tiled=T...]
    all_to_all x6 -> x0, waiting for transfers between devices: 45.8 us -> none  [the longest x1 16.1 us: per_device(): lax.all_to_all(d_spatial, 'seq', split_axis=1, concat_axis=2, tiled=True)]
    dot_general x14 -> x0, matrix products: 43.1 us -> none  [the longest x3 10.2 us: temporal_block(): jnp.einsum('cfphd,cgphd->cphfg', query_norm, key_norm, preferred_element_...]
    unnamed x110 -> x16, local copies, waits for them, and re-layouts: 47.5 us -> 8.08 us
    unnamed x3 -> x0, other arithmetic: 20 us -> none
  transfers between devices with their start and end apart: 9 -> 0, of which waited for: 7 -> 0; matrix products, arithmetic and copies ran while one was open for 24% -> 0% of each run, Pallas kernels for 0% -> 0%
where the time goes in v1:
time: 149 us
  Pallas kernels  140 us (94%)
  local copies, waits for them, and re-layouts  8.08 us (5%)
    pallas_call x1, Pallas kernels, per_device(): pl.pallas_call(kernel, out_shape=(*(jax.ShapeDtypeStruct(frame, BF16) for...  140 us
    unnamed x16, local copies, waits for them, and re-layouts  8.08 us

profile of v1, /device:TPU:1, one launch (start us, length us, event | category | flops | bytes accessed | tf_op | source)
XLA Modules:
  0.0 148.8 jit_solution(4607162655646473925)
XLA Ops:
  0.6 140.0 %shard_map.127 = (bf16[256,1536]{1,0:T(8,128)(2,1)}, bf16[256,1536]{1,0:T(8,128)(2,1)}, bf16[256,1536]{1,0:T(8,128)(2,1)}, bf16[32,8,1536]{2,1,0:T(8,128)(2,1)},...) custom-call(s32[2,2]{1,0:T(2,128)} %bitcast.23, bf16[256,1536]{1,0:T(8,128)(2,1)} %bitcast.17, ...), custom_call_target="tpu_custom_call" | custom-call | tf_op jit(solution)/shard_map/pallas_call | solution.py:414
  140.7 0.0 copy-start.3
  140.7 2.1 %copy.20 = bf16[1,1,256,1536]{3,2,1,0:T(8,128)(2,1)} copy(bf16[1,1,256,1536]{3,2,1,0:T(8,128)(2,1)} %bitcast.16) | data formatting | bytes 1572864
  142.8 0.0 copy-done.3
  142.8 0.0 copy-start.2
  142.8 0.9 copy.21
  143.7 0.5 copy-done.2
  144.3 0.0 copy-start.1
  144.3 0.9 copy.22
  145.1 0.5 copy-done.1
  145.7 0.0 copy-start
  145.7 0.9 copy.23
  146.5 0.5 copy-done
  147.1 0.0 copy-start.4
  147.1 0.9 copy.24
  148.0 0.1 copy-done.4
  148.1 0.7 copy.25
Async XLA Ops:
  140.7 2.1 %copy-start.3 = (bf16[256,1536]{1,0:T(8,128)(2,1)S(1)}, bf16[256,1536]{1,0:T(8,128)(2,1)}, u32[]{:S(2)}) copy-start(bf16[256,1536]{1,0:T(8,128)(2,1)} %get-tuple-element.13) | copy-start | bytes 2359300
  142.8 1.4 copy-start.2
  144.3 1.4 copy-start.1
  145.7 1.4 copy-start
  147.1 1.0 copy-start.4

commit v2 on v1

v2 whole, which is shorter than its diff:
```python
import math

import jax
import jax.numpy as jnp
from jax import lax
from jax.experimental import pallas as pl
from jax.experimental.pallas import tpu as pltpu
from jax.sharding import PartitionSpec as P

HEADS = 12
HEAD_DIM = 128
TILE = 128
WIDTH = HEADS * HEAD_DIM
NX, NY, NZ = 4, 4, 8
SEQ = NZ * NY
ROWS = 48
PATCH = 256
PAIR = 2 * HEAD_DIM
PAIRS = WIDTH // PAIR
CHUNK = 512
THIRDS = WIDTH // CHUNK
COLS = WIDTH // NX
SCALE = 1.0 / math.sqrt(HEAD_DIM)
SCALE2 = SCALE * math.log2(math.e)
EPS = 1e-06
MESH = pl.DeviceIdType.MESH
F32 = jnp.float32
BF16 = jnp.bfloat16


def dot(a, b, contract):
    return lax.dot_general(a, b, ((contract[:1], contract[1:]), ((), ())), preferred_element_type=F32)


def inverse_rms(a):
    return lax.rsqrt(jnp.mean(a * a, axis=-1, keepdims=True) + EPS)


def norm_back(grad, normed, inverse):
    return (inverse * SCALE) * (grad - normed * jnp.mean(grad * normed, axis=-1, keepdims=True))


def softmax(q_norm, k_norm, mask):
    exps = jnp.exp2(dot(q_norm, k_norm, (1, 1)) * SCALE2) * mask
    return exps * (1.0 / jnp.sum(exps, axis=-1, keepdims=True))


def attention_back(weights, weights_b, q, k, qn, kn, rq, rk, qn_b, kn_b, v, grad):
    d_weights = dot(grad, v, (1, 1))
    delta = jnp.sum(weights * d_weights, axis=-1, keepdims=True)
    d_scores = (weights * (d_weights - delta)).astype(BF16)
    d_v = dot(weights_b, grad, (0, 0))
    d_q = norm_back(dot(d_scores, kn_b, (1, 0)), qn, rq)
    d_k = norm_back(dot(d_scores, qn_b, (0, 0)), kn, rk)
    return d_q, d_k, d_v


def wait_for(ref, sem):
    pltpu.make_async_copy(ref, ref, sem).wait()


def kernel(
    tile_ref, q_in, k_in, v_in, tk_ref, tv_ref, w_in_ref, og_in,
    dq_ref, dk_ref, dv_ref, dtk_ref, dtv_ref, dw_ref,
    q_ref, k_ref, v_ref, og_ref, w_ref, weight, mask, tmask, spatial, k_buf, v_buf, s_buf, s_mat, d_mat, attn,
    dk_send, dv_send, ds_send, ds_buf,
    part, core_in, x_in, x_sum, y_in, y_sum, z_in, final,
    load, send, a2a_in, tk_in, tv_in, tk_out, tv_out, s_out, dk_out, dv_out, wz_in, wy_in, wx_in, wc_in,
    core_sem, x_sem, y_sem, z_sem, out_sem, g_send,
):
    d = lax.axis_index("dp")
    s = lax.axis_index("seq")
    x, c = d // 2, d % 2
    z, y = s // NY, s % NY
    sibling = {"dp": x * 2 + 1 - c}
    active = y % 2 == c
    idle = y % 2 != c

    def seq_peer(o):
        return lax.rem(s + o, SEQ)

    def x_peer(o):
        return {"dp": lax.rem(x + o, NX) * 2 + c}

    def y_peer(o):
        return {"seq": z * NY + lax.rem(y + o, NY)}

    def z_peer(o):
        return {"seq": lax.rem(z + o, NZ) * NY + y}

    def remote(src, dst, send_sem, recv_sem, device):
        pltpu.make_async_remote_copy(
            src, dst, send_sem, recv_sem, device_id=device, device_id_type=MESH
        ).start()

    def exchange(src, dst, lanes, send_sem, recv_sem):
        pltpu.make_async_copy(src.at[s, :, lanes], dst.at[s, :, lanes], recv_sem).start()

        @pl.loop(1, SEQ)
        def _(o):
            j = seq_peer(o)
            remote(src.at[j, :, lanes], dst.at[s, :, lanes], send_sem, recv_sem, {"seq": j})

    def lanes_of(n, width):
        return pl.ds(pl.multiple_of(n * width, width), width)

    own_cols = lanes_of(x, COLS)

    def chunk_of(g):
        return lanes_of(g, CHUNK)

    loads = ((w_in_ref, w_ref), (q_in, q_ref), (k_in, k_ref), (v_in, v_ref), (og_in, og_ref))
    for i, (src, dst) in enumerate(loads):
        pltpu.make_async_copy(src, dst, load.at[i]).start()

    wait_for(w_ref, load.at[0])
    weight[z, y] = w_ref[...]

    barrier = pltpu.get_barrier_semaphore()

    @pl.loop(1, SEQ)
    def _(o):
        pl.semaphore_signal(barrier, inc=1, device_id={"seq": seq_peer(o)}, device_id_type=MESH)

    @pl.loop(1, 2 * NX)
    def _(o):
        pl.semaphore_signal(barrier, inc=1, device_id={"dp": lax.rem(d + o, 2 * NX)}, device_id_type=MESH)

    ones = jnp.ones((TILE, TILE), F32)
    for a in range(2):
        for b in range(2):
            value = 1.0 if a == b else jnp.where(tile_ref[a, b] == 1, 1.0, 0.0).astype(F32)
            mask[a * TILE:(a + 1) * TILE, b * TILE:(b + 1) * TILE] = ones * value
    row = lax.broadcasted_iota(jnp.int32, (PATCH, PATCH), 0)
    col = lax.broadcasted_iota(jnp.int32, (PATCH, PATCH), 1)
    tmask[...] = jnp.where(row % 8 == col % 8, 1.0, 0.0).astype(F32)

    pl.semaphore_wait(barrier, SEQ - 1 + 2 * NX - 1)

    def cols_of(xs, g):
        return pl.ds(pl.multiple_of(xs * COLS + g * HEAD_DIM, HEAD_DIM), HEAD_DIM)

    for g in range(THIRDS):
        @pl.when(active)
        def _():
            src = weight.at[z, y, :, cols_of(x, g)]

            @pl.loop(1, NZ)
            def _(o):
                remote(src, src, send.at[0], wz_in.at[g], z_peer(o))

    exchange(tk_ref, k_buf, chunk_of(0), tk_out.at[0], tk_in.at[0])

    for i in (1, 2, 3):
        wait_for(loads[i][1], load.at[i])

    @pl.loop(0, PAIRS)
    def _(n):
        lanes = lanes_of(n, PAIR)
        q2, k2 = q_ref[:, lanes].astype(F32), k_ref[:, lanes].astype(F32)
        v2 = v_ref[:, lanes]
        outs = []
        for h in range(2):
            cut = slice(h * HEAD_DIM, (h + 1) * HEAD_DIM)
            q, k = q2[:, cut], k2[:, cut]
            qn = (q * inverse_rms(q)).astype(BF16)
            kn = (k * inverse_rms(k)).astype(BF16)
            weights = softmax(qn, kn, mask[...]).astype(BF16)
            attn[2 * n + h] = weights
            outs.append(dot(weights, v2[:, cut], (1, 0)))
        out = jnp.concatenate(outs, axis=1)
        spatial[:, :, lanes] = out.reshape(SEQ, 8, PAIR).astype(BF16)

        @pl.when(n % 2 == 1)
        def _():
            exchange(spatial, s_buf, chunk_of(n // 2), s_out.at[n // 2], a2a_in.at[1])

    def sent(sem):
        wait_for(k_buf.at[pl.ds(0, SEQ - 1), :, pl.ds(0, CHUNK)], sem)

    def send_k(g):
        exchange(tk_ref, k_buf, chunk_of(g), tk_out.at[g], tk_in.at[g])

    def send_v(g):
        exchange(tv_ref, v_buf, chunk_of(g), tv_out.at[g], tv_in.at[g])

    for g in range(THIRDS):
        @pl.when(active)
        def _():
            wait_for(weight.at[pl.ds(0, NZ - 1), y, :, cols_of(x, g)], wz_in.at[g])
            src = weight.at[:, y, :, cols_of(x, g)]

            @pl.loop(1, NY)
            def _(o):
                remote(src, src, send.at[1], wy_in.at[g], y_peer(o))

    sent(tk_out.at[0])
    send_v(0)

    for g in range(THIRDS):
        @pl.when(active)
        def _():
            wait_for(weight.at[:, 0, :, cols_of(x, g)], wy_in.at[g])

        @pl.when(idle)
        def _():
            wait_for(weight.at[:, pl.ds(0, 2), :, cols_of(x, g)], wy_in.at[g])

        for h in range(2):
            src = weight.at[:, c + 2 * h, :, cols_of(x, g)]

            @pl.loop(1, NX)
            def _(o):
                remote(src, src, send.at[2], wx_in.at[g, o - 1], x_peer(o))

            remote(src, src, send.at[3], wc_in, sibling)

    sent(s_out.at[0])
    send_k(1)
    sent(s_out.at[1])
    send_v(1)

    for g in range(THIRDS):
        for o in (1, 3, 2):
            cols = cols_of(lax.rem(x + NX - o, NX), g)
            wait_for(weight.at[:, pl.ds(0, 2), :, cols], wx_in.at[g, o - 1])
            for h in range(2):
                src = weight.at[:, c + 2 * h, :, cols]
                remote(src, src, send.at[3], wc_in, sibling)
        if g == 0:
            sent(s_out.at[2])
            send_k(2)
        if g == 1:
            sent(tv_out.at[0])
            send_v(2)

    wait_for(s_buf, a2a_in.at[1])
    for n in range(PAIRS):
        lanes = slice(n * PAIR, (n + 1) * PAIR)
        s_mat[:, lanes] = s_buf[:, :, lanes].astype(F32).reshape(PATCH, PAIR).astype(BF16)
    wait_for(weight.at[:, pl.ds(0, 2)], wc_in)
    wait_for(og_ref, load.at[4])

    def part_step(g):
        cols = d_mat[:, chunk_of(g)]

        @pl.loop(0, NZ // 2)
        def _(m):
            block = dot(s_mat[:, lanes_of(m, 2 * NY * ROWS)], cols, (0, 0))
            part[g, pl.ds(2 * m, 2)] = block.reshape(2, NY, ROWS, CHUNK).astype(BF16)

        for h in range(2):
            remote(part.at[g, :, 1 - c + 2 * h], core_in.at[g, h], g_send.at[0], core_sem.at[g], sibling)

    def x_step(g):
        wait_for(core_in.at[g], core_sem.at[g])
        for h in range(2):
            own = part[g, :, c + 2 * h].astype(F32) + core_in[g, h].astype(F32)
            part[g, :, c + 2 * h] = own.astype(BF16)

            @pl.loop(1, NX)
            def _(o):
                to = lax.rem(x + o, NX)
                remote(
                    part.at[g, :, c + 2 * h, :, lanes_of(to, HEAD_DIM)], x_in.at[g, o - 1, h],
                    g_send.at[1], x_sem.at[g], x_peer(o),
                )

    def y_step(g):
        wait_for(x_in.at[g], x_sem.at[g])
        for h in range(2):
            total = part[g, :, c + 2 * h, :, lanes_of(x, HEAD_DIM)].astype(F32)
            for o in range(NX - 1):
                total = total + x_in[g, o, h].astype(F32)
            x_sum[g, h] = total.astype(BF16)
            owner = c + 2 * h

            @pl.when(y != owner)
            def _():
                away = lax.rem(y - owner + NY, NY)
                remote(x_sum.at[g, h], y_in.at[g, away - 1], g_send.at[2], y_sem.at[g], {"seq": z * NY + owner})

    def z_step(g):
        @pl.when(active)
        def _():
            wait_for(y_in.at[g], y_sem.at[g])
            total = x_sum[g, y // 2].astype(F32)
            for o in range(NY - 1):
                total = total + y_in[g, o].astype(F32)
            y_sum[g] = total.astype(BF16)

            @pl.loop(1, NZ)
            def _(o):
                remote(
                    y_sum.at[g, lax.rem(z + o, NZ)], z_in.at[g, o - 1], g_send.at[3], z_sem.at[g], z_peer(o)
                )

    def out_step(g):
        @pl.when(active)
        def _():
            wait_for(z_in.at[g], z_sem.at[g])
            total = y_sum[g, z].astype(F32)
            for o in range(NZ - 1):
                total = total + z_in[g, o].astype(F32)
            final[g] = total.astype(BF16)
            dst = dw_ref.at[:, pl.ds(pl.multiple_of(g * CHUNK + x * HEAD_DIM, HEAD_DIM), HEAD_DIM)]
            pltpu.make_async_copy(final.at[g], dst, out_sem).start()

            @pl.loop(1, 2 * NX)
            def _(o):
                remote(final.at[g], dst, g_send.at[4], out_sem, {"dp": lax.rem(d + o, 2 * NX)})

    @pl.loop(0, PAIRS)
    def _(n):
        lanes = lanes_of(n, PAIR)

        @pl.when(n % 2 == 0)
        def _():
            g = n // 2
            wait_for(k_buf.at[:, :, chunk_of(g)], tk_in.at[g])
            wait_for(v_buf.at[:, :, chunk_of(g)], tv_in.at[g])

        rows = weight[:, :, :, lanes].reshape(WIDTH, PAIR)
        q2 = dot(s_mat[...], rows, (1, 0)).astype(BF16).astype(F32)
        k2 = k_buf[:, :, lanes].astype(F32).reshape(PATCH, PAIR)
        v2 = v_buf[:, :, lanes].astype(F32).reshape(PATCH, PAIR).astype(BF16)
        g2 = og_ref[:, :, lanes].astype(F32).reshape(PATCH, PAIR).astype(BF16)
        d_qs, d_ks, d_vs = [], [], []
        for h in range(2):
            cut = slice(h * HEAD_DIM, (h + 1) * HEAD_DIM)
            q, k = q2[:, cut], k2[:, cut]
            rq, rk = inverse_rms(q), inverse_rms(k)
            qn, kn = q * rq, k * rk
            qn_b, kn_b = qn.astype(BF16), kn.astype(BF16)
            weights = softmax(qn_b, kn_b, tmask[...])
            d_q, d_k, d_v = attention_back(
                weights, weights.astype(BF16), q, k, qn, kn, rq, rk, qn_b, kn_b, v2[:, cut], g2[:, cut]
            )
            d_qs.append(d_q)
            d_ks.append(d_k)
            d_vs.append(d_v)
        d_mat[:, lanes] = jnp.concatenate(d_qs, axis=1).astype(BF16)
        dk_send[:, :, lanes] = jnp.concatenate(d_ks, axis=1).reshape(SEQ, 8, PAIR).astype(BF16)
        dv_send[:, :, lanes] = jnp.concatenate(d_vs, axis=1).reshape(SEQ, 8, PAIR).astype(BF16)

        @pl.when(n % 2 == 1)
        def _():
            part_step(n // 2)

        @pl.when(n == 3)
        def _():
            x_step(0)

        @pl.when(n == 5)
        def _():
            x_step(1)

        @pl.when(n == 1)
        def _():
            first = pl.ds(0, CHUNK)
            exchange(dk_send, dtk_ref, first, dk_out.at[0], a2a_in.at[3])
            exchange(dv_send, dtv_ref, first, dv_out.at[0], a2a_in.at[4])

    @pl.loop(0, NZ // 2)
    def _(m):
        rows = weight[pl.ds(2 * m, 2)].reshape(2 * NY * ROWS, WIDTH)
        out = dot(d_mat[...], rows, (1, 1))
        lanes = lanes_of(m, 2 * NY * ROWS)
        ds_send[:, :, lanes] = out.reshape(SEQ, 8, 2 * NY * ROWS).astype(BF16)
        exchange(ds_send, ds_buf, lanes, send.at[4], a2a_in.at[5])

    def send_back(g):
        exchange(dk_send, dtk_ref, chunk_of(g), dk_out.at[g], a2a_in.at[3])
        exchange(dv_send, dtv_ref, chunk_of(g), dv_out.at[g], a2a_in.at[4])

    x_step(2)
    sent(dk_out.at[0])
    sent(dv_out.at[0])
    send_back(1)
    y_step(0)
    y_step(1)
    z_step(0)
    send_back(2)
    y_step(2)
    z_step(1)

    wait_for(ds_buf, a2a_in.at[5])

    @pl.loop(0, PAIRS)
    def _(n):
        lanes = lanes_of(n, PAIR)
        q2, k2 = q_ref[:, lanes].astype(F32), k_ref[:, lanes].astype(F32)
        v2 = v_ref[:, lanes]
        g2 = ds_buf[:, :, lanes].astype(F32).reshape(PATCH, PAIR).astype(BF16)
        d_qs, d_ks, d_vs = [], [], []
        for h in range(2):
            cut = slice(h * HEAD_DIM, (h + 1) * HEAD_DIM)
            q, k = q2[:, cut], k2[:, cut]
            rq, rk = inverse_rms(q), inverse_rms(k)
            qn, kn = q * rq, k * rk
            weights = attn[2 * n + h]
            d_q, d_k, d_v = attention_back(
                weights.astype(F32), weights, q, k, qn, kn, rq, rk, qn.astype(BF16), kn.astype(BF16),
                v2[:, cut], g2[:, cut],
            )
            d_qs.append(d_q)
            d_ks.append(d_k)
            d_vs.append(d_v)
        dq_ref[:, lanes] = jnp.concatenate(d_qs, axis=1).astype(BF16)
        dk_ref[:, lanes] = jnp.concatenate(d_ks, axis=1).astype(BF16)
        dv_ref[:, lanes] = jnp.concatenate(d_vs, axis=1).astype(BF16)

        @pl.when(n == 1)
        def _():
            z_step(2)
            out_step(0)

        @pl.when(n == 3)
        def _():
            out_step(1)

    out_step(2)

    wait_for(dtk_ref, a2a_in.at[3])
    wait_for(dtv_ref, a2a_in.at[4])

    wait_for(dw_ref, out_sem)

    for sem in (tk_out.at[1], tk_out.at[2], tv_out.at[1], tv_out.at[2]):
        sent(sem)
    for sem in (dk_out.at[1], dk_out.at[2], dv_out.at[1], dv_out.at[2]):
        sent(sem)
    wait_for(ds_buf.at[pl.ds(0, SEQ - 1)], send.at[4])
    wait_for(weight.at[:, pl.ds(0, 2), :, pl.ds(0, 3 * COLS)], send.at[2])
    wait_for(weight.at[:, pl.ds(0, 2)], send.at[3])
    wait_for(core_in, g_send.at[0])
    wait_for(x_in, g_send.at[1])

    @pl.when(active)
    def _():
        wait_for(weight.at[pl.ds(0, NZ - 1), y, :, own_cols], send.at[0])
        wait_for(weight.at[:, 0, :, pl.ds(0, 3 * COLS)], send.at[1])
        wait_for(x_sum.at[:, 0], g_send.at[2])
        wait_for(z_in, g_send.at[3])
        wait_for(z_in, g_send.at[4])

    @pl.when(idle)
    def _():
        wait_for(x_sum, g_send.at[2])


def store(*refs):
    copies = [pltpu.make_async_copy(refs[i], refs[6 + i], refs[12].at[i]) for i in range(6)]
    for copy in copies:
        copy.start()
    for copy in copies:
        copy.wait()


def per_device(
    queries, keys_spatial, values_spatial, temporal_keys, temporal_values, tile_mask, query_weight, out_grad
):
    frame = (PATCH, WIDTH)
    blocks = (SEQ, 8, WIDTH)
    vmem = pl.BlockSpec(memory_space=pltpu.VMEM)
    smem = pl.BlockSpec(memory_space=pltpu.SMEM)
    anywhere = pl.BlockSpec(memory_space=pl.ANY)
    dma = pltpu.SemaphoreType.DMA

    def buf(*shape, kind=BF16):
        return pltpu.VMEM(shape, kind)

    results = pl.pallas_call(
        kernel,
        out_shape=(
            *(pltpu.VMEM(frame, BF16) for _ in range(3)),
            *(pltpu.VMEM(blocks, BF16) for _ in range(2)),
            pltpu.VMEM((ROWS, WIDTH), BF16),
        ),
        in_specs=[smem] + [anywhere] * 7,
        out_specs=(vmem,) * 6,
        scratch_shapes=[
            buf(*frame), buf(*frame), buf(*frame), buf(*blocks), buf(ROWS, WIDTH),
            buf(NZ, NY, ROWS, WIDTH),
            buf(PATCH, PATCH, kind=F32),
            buf(PATCH, PATCH, kind=F32),
            buf(*blocks), buf(*blocks), buf(*blocks), buf(*blocks),
            buf(*frame), buf(*frame),
            buf(HEADS, PATCH, PATCH),
            buf(*blocks), buf(*blocks), buf(*blocks), buf(*blocks),
            buf(THIRDS, NZ, NY, ROWS, CHUNK),
            buf(THIRDS, 2, NZ, ROWS, CHUNK),
            buf(THIRDS, NX - 1, 2, NZ, ROWS, HEAD_DIM),
            buf(THIRDS, 2, NZ, ROWS, HEAD_DIM),
            buf(THIRDS, NY - 1, NZ, ROWS, HEAD_DIM),
            buf(THIRDS, NZ, ROWS, HEAD_DIM),
            buf(THIRDS, NZ - 1, ROWS, HEAD_DIM),
            buf(THIRDS, ROWS, HEAD_DIM),
            dma((5,)), dma((5,)), dma((6,)), *(dma((THIRDS,)) for _ in range(9)), dma((THIRDS, NX - 1)), dma,
            dma((THIRDS,)), dma((THIRDS,)), dma((THIRDS,)), dma((THIRDS,)), dma, dma((5,)),
        ],
        compiler_params=pltpu.CompilerParams(
            collective_id=0, has_side_effects=True, vmem_limit_bytes=56 << 20
        ),
    )(
        tile_mask.reshape(2, 2),
        queries.reshape(frame),
        keys_spatial.reshape(frame),
        values_spatial.reshape(frame),
        temporal_keys.reshape(blocks),
        temporal_values.reshape(blocks),
        query_weight,
        out_grad.reshape(blocks),
    )
    d_q, d_k, d_v, d_tk, d_tv, d_w = pl.pallas_call(
        store,
        out_shape=tuple(jax.ShapeDtypeStruct(a.shape, a.dtype) for a in results),
        in_specs=[anywhere] * 6,
        out_specs=(anywhere,) * 6,
        scratch_shapes=[dma((6,))],
        compiler_params=pltpu.CompilerParams(vmem_limit_bytes=1 << 20),
    )(*results)
    whole = (1, 1, PATCH, WIDTH)
    return (*(a.reshape(whole) for a in (d_q, d_k, d_v, d_tk, d_tv)), d_w)


def solution(mesh):
    framed = P("dp", "seq", None, None)
    return jax.shard_map(
        per_device,
        mesh=mesh,
        in_specs=(framed,) * 6 + (P("seq", None), P("dp", None, "seq", None)),
        out_specs=(framed,) * 5 + (P("seq", None),),
        check_vma=False,
    )
```

time: 149 us -> 132 us (0.89)
  Pallas kernels: 140 us -> 131 us
  local copies, waits for them, and re-layouts: 8.08 us -> 0 us
    pallas_call x1 -> x2, Pallas kernels: 140 us -> 131 us  [the longest x1 129 us: per_device(): pl.pallas_call(kernel, out_shape=(*(pltpu.VMEM(frame, BF16) for _ in rang...]
    unnamed x16 -> x0, local copies, waits for them, and re-layouts: 8.08 us -> none
where the time goes in v2:
time: 132 us
  Pallas kernels  131 us (99%)
    pallas_call x1, Pallas kernels, per_device(): pl.pallas_call(kernel, out_shape=(*(pltpu.VMEM(frame, BF16) for _ in rang...  129 us

profile of v2, /device:TPU:1, one launch (start us, length us, event | category | flops | bytes accessed | tf_op | source)
XLA Modules:
  0.0 131.6 jit_solution(13314137650134228456)
XLA Ops:
  0.6 128.9 %shard_map.127 = (bf16[256,1536]{1,0:T(8,128)(2,1)S(1)}, bf16[256,1536]{1,0:T(8,128)(2,1)S(1)}, bf16[256,1536]{1,0:T(8,128)(2,1)S(1)}, bf16[32,8,1536]{2,1,0:T(8...) custom-call(s32[2,2]{1,0:T(2,128)} %bitcast.18, bf16[256,1536]{1,0:T(8,128)(2,1)} %bitcast.12, ...), custom_call_target="tpu_custom_call" | custom-call | tf_op jit(solution)/shard_map/pallas_call | solution.py:473
  129.6 2.0 %shard_map.128 = (bf16[256,1536]{1,0:T(8,128)(2,1)}, bf16[256,1536]{1,0:T(8,128)(2,1)}, bf16[256,1536]{1,0:T(8,128)(2,1)}, bf16[32,8,1536]{2,1,0:T(8,128)(2,1)},...) custom-call(bf16[256,1536]{1,0:T(8,128)(2,1)S(1)} %get-tuple-element.18.refs_0_, ...), custom_call_target="tpu_custom_call" | custom-call | tf_op jit(solution)/shard_map/pallas_call | solution.py:515

commit v3 on v2

--- a/solution.py
+++ b/solution.py
@@ -374,15 +374,17 @@
         exchange(dv_send, dtv_ref, chunk_of(g), dv_out.at[g], a2a_in.at[4])
 
     x_step(2)
+    y_step(0)
+    y_step(1)
     sent(dk_out.at[0])
     sent(dv_out.at[0])
     send_back(1)
-    y_step(0)
-    y_step(1)
     z_step(0)
-    send_back(2)
     y_step(2)
     z_step(1)
+    z_step(2)
+    wait_for(ds_buf.at[pl.ds(0, SEQ - 1)], send.at[4])
+    send_back(2)
 
     wait_for(ds_buf, a2a_in.at[5])
 
@@ -412,7 +414,6 @@
 
         @pl.when(n == 1)
         def _():
-            z_step(2)
             out_step(0)
 
         @pl.when(n == 3)
@@ -430,7 +431,6 @@
         sent(sem)
     for sem in (dk_out.at[1], dk_out.at[2], dv_out.at[1], dv_out.at[2]):
         sent(sem)
-    wait_for(ds_buf.at[pl.ds(0, SEQ - 1)], send.at[4])
     wait_for(weight.at[:, pl.ds(0, 2), :, pl.ds(0, 3 * COLS)], send.at[2])
     wait_for(weight.at[:, pl.ds(0, 2)], send.at[3])
     wait_for(core_in, g_send.at[0])

time: 132 us -> 127 us (0.962)
  Pallas kernels: 131 us -> 126 us
    pallas_call x1, Pallas kernels: 129 us -> 124 us  [per_device(): pl.pallas_call(kernel, out_shape=(*(pltpu.VMEM(frame, BF16) for _ in rang...]
where the time goes in v3:
time: 127 us; the launch traced here: 126 us
  Pallas kernels  126 us (99%)
    pallas_call x1, Pallas kernels, per_device(): pl.pallas_call(kernel, out_shape=(*(pltpu.VMEM(frame, BF16) for _ in rang...  124 us

profile of v3, /device:TPU:1, one launch (start us, length us, event | category | flops | bytes accessed | tf_op | source)
XLA Modules:
  0.0 126.2 jit_solution(9997466010505805256)
XLA Ops:
  0.6 123.5 %shard_map.127 = (bf16[256,1536]{1,0:T(8,128)(2,1)S(1)}, bf16[256,1536]{1,0:T(8,128)(2,1)S(1)}, bf16[256,1536]{1,0:T(8,128)(2,1)S(1)}, bf16[32,8,1536]{2,1,0:T(8...) custom-call(s32[2,2]{1,0:T(2,128)} %bitcast.18, bf16[256,1536]{1,0:T(8,128)(2,1)} %bitcast.12, ...), custom_call_target="tpu_custom_call" | custom-call | tf_op jit(solution)/shard_map/pallas_call | solution.py:473
  124.2 2.0 %shard_map.128 = (bf16[256,1536]{1,0:T(8,128)(2,1)}, bf16[256,1536]{1,0:T(8,128)(2,1)}, bf16[256,1536]{1,0:T(8,128)(2,1)}, bf16[32,8,1536]{2,1,0:T(8,128)(2,1)},...) custom-call(bf16[256,1536]{1,0:T(8,128)(2,1)S(1)} %get-tuple-element.18.refs_0_, ...), custom_call_target="tpu_custom_call" | custom-call | tf_op jit(solution)/shard_map/pallas_call | solution.py:515

commit v4 on v3

--- a/solution.py
+++ b/solution.py
@@ -361,6 +361,8 @@
             exchange(dk_send, dtk_ref, first, dk_out.at[0], a2a_in.at[3])
             exchange(dv_send, dtv_ref, first, dv_out.at[0], a2a_in.at[4])
 
+    x_step(2)
+
     @pl.loop(0, NZ // 2)
     def _(m):
         rows = weight[pl.ds(2 * m, 2)].reshape(2 * NY * ROWS, WIDTH)
@@ -373,7 +375,6 @@
         exchange(dk_send, dtk_ref, chunk_of(g), dk_out.at[g], a2a_in.at[3])
         exchange(dv_send, dtv_ref, chunk_of(g), dv_out.at[g], a2a_in.at[4])
 
-    x_step(2)
     y_step(0)
     y_step(1)
     sent(dk_out.at[0])

time: 127 us -> 132 us (1.039)
  Pallas kernels: 126 us -> 131 us
    pallas_call x1, Pallas kernels: 124 us -> 129 us  [per_device(): pl.pallas_call(kernel, out_shape=(*(pltpu.VMEM(frame, BF16) for _ in rang...]
where the time goes in v4:
time: 132 us
  Pallas kernels  131 us (99%)
    pallas_call x1, Pallas kernels, per_device(): pl.pallas_call(kernel, out_shape=(*(pltpu.VMEM(frame, BF16) for _ in rang...  129 us

profile of v4, /device:TPU:1, one launch (start us, length us, event | category | flops | bytes accessed | tf_op | source)
XLA Modules:
  0.0 132.0 jit_solution(1850692817599977347)
XLA Ops:
  0.6 129.3 %shard_map.127 = (bf16[256,1536]{1,0:T(8,128)(2,1)S(1)}, bf16[256,1536]{1,0:T(8,128)(2,1)S(1)}, bf16[256,1536]{1,0:T(8,128)(2,1)S(1)}, bf16[32,8,1536]{2,1,0:T(8...) custom-call(s32[2,2]{1,0:T(2,128)} %bitcast.18, bf16[256,1536]{1,0:T(8,128)(2,1)} %bitcast.12, ...), custom_call_target="tpu_custom_call" | custom-call | tf_op jit(solution)/shard_map/pallas_call | solution.py:474
  130.0 2.0 %shard_map.128 = (bf16[256,1536]{1,0:T(8,128)(2,1)}, bf16[256,1536]{1,0:T(8,128)(2,1)}, bf16[256,1536]{1,0:T(8,128)(2,1)}, bf16[32,8,1536]{2,1,0:T(8,128)(2,1)},...) custom-call(bf16[256,1536]{1,0:T(8,128)(2,1)S(1)} %get-tuple-element.18.refs_0_, ...), custom_call_target="tpu_custom_call" | custom-call | tf_op jit(solution)/shard_map/pallas_call | solution.py:516
